TPU v7x, 32 devices: a whole 2x2x4 slice. The times are simulated.
32 devices in a mesh: dp: 2 (over y), mp: 16 (over z, x, core).
Axes of the slice: x: 2, y: 2, z: 4, core: 2. Of those that a mesh axis runs over, the one named last changes fastest.
Arguments:
- query: bfloat16 [512, 1024], P('dp', 'mp'), may hold values from -0.75 to 0.75
- kv_cache: bfloat16 [1024, 2048], P('dp', 'mp'), may hold values from -4 to 4, as said below
- out_grad: bfloat16 [512, 1024], P('dp', 'mp'), may hold values from -384 to 384
- source_lengths: int32 [2, 8], P('dp'), may hold values from 1 to 128, 512 in all within a row
- target_lengths: int32 [2, 8], P('dp'), may hold values from 1 to 64, 256 in all within a row
- low_rank: bfloat16 [1024, 32], P(('dp', 'mp')), may hold values from -0.125 to 0.125
- adapter_up_matrix: bfloat16 [32, 1024], replicated, may hold values from -0.1875 to 0.1875
Outputs:
- query_grad: bfloat16 [512, 1024], P('dp', 'mp')
- key_gradient: bfloat16 [1024, 1024], P(('dp', 'mp'))
- value_grad: bfloat16 [1024, 1024], P(('dp', 'mp'))
- low_rank_gradient: float32 [1024, 32], P(('dp', 'mp'))
- adapter_up_gradient: float32 [1024, 32], P(('dp', 'mp'))
Inputs may be any that keep to these rules, and one draw needn't show every extreme that they name: `source_lengths`: each row sums to 512; its largest entry is exactly 128. `target_lengths`: each row sums to 256; its largest entry is exactly 64. `kv_cache`: the key columns lie within -0.75 to 0.75.
All inputs are finite; a program needn't handle non-finite values.
Results may differ from a plain program's by a relative error of at most 0.0053.
Values may be sent and summed in bfloat16 or wider, within the bound.
No kernel may reach another device: no remote copies, remote signals or barrier semaphores. Data moves between devices by JAX's collectives and lax.ppermute only.
A program may use at most 64 MiB of HBM per device.

v0:
```python
import functools

import jax
import jax.numpy as jnp
from jax import lax
from jax.experimental import pallas as pl
from jax.experimental.pallas import tpu as pltpu
from jax.sharding import PartitionSpec as P

HS = 64
LANES = 128
CUT = 16

adapter_factor = 2.0

NT = (((1,), (1,)), ((), ()))
TN = (((0,), (0,)), ((), ()))


def dot(left, right, dims):
    return lax.dot_general(left, right, dims, preferred_element_type=jnp.float32)


def source_range(source_ref, target_ref, count):
    position = lax.broadcasted_iota(jnp.int32, (1, count), 1)
    first = jnp.zeros((1, count), jnp.int32)
    last = jnp.zeros((1, count), jnp.int32)
    target_start = jnp.int32(0)
    source_start = jnp.int32(0)
    for i in range(source_ref.shape[1]):
        source_end = source_start + source_ref[0, i]
        inside = position >= target_start
        first = jnp.where(inside, source_start, first)
        last = jnp.where(inside, source_end, last)
        target_start = target_start + target_ref[0, i]
        source_start = source_end
    return first, last


def attention_kernel(
    source_any, target_any, query_any, grad_any, kv_any, low_any,
    query_grad_ref, sent_ref,
    source_ref, target_ref, query_ref, grad_ref, kv_ref, low_ref, sems,
):
    pairs = [
        (kv_any, kv_ref), (query_any, query_ref), (grad_any, grad_ref),
        (source_any, source_ref), (target_any, target_ref), (low_any, low_ref),
    ]
    copies = [
        pltpu.make_async_copy(here, there, sems.at[i]) for i, (here, there) in enumerate(pairs)
    ]
    for copy in copies:
        copy.start()
    for copy in copies:
        copy.wait()
    tgt_count = query_ref.shape[1]
    both = kv_ref[...]
    query_t = query_ref[...]
    grad_t = grad_ref[...]
    blank = jnp.zeros_like(query_t)
    query_wide = jnp.concatenate([query_t, blank], axis=0)
    grad_wide = jnp.concatenate([blank, grad_t], axis=0)
    scores = jnp.dot(both, query_wide, preferred_element_type=jnp.float32)
    dprob = jnp.dot(both, grad_wide, preferred_element_type=jnp.float32)
    first, last = source_range(source_ref, target_ref, tgt_count)
    position = lax.broadcasted_iota(jnp.int32, scores.shape, 0)
    allowed = jnp.logical_and(position >= first, position < last)
    expo = jnp.where(allowed, jnp.exp(scores), 0.0)
    total = jnp.sum(expo, axis=0, keepdims=True)
    delta = jnp.sum(expo * dprob, axis=0, keepdims=True) / total
    prob = expo * (1.0 / total)
    prob_low = prob.astype(jnp.bfloat16)
    dscore = (prob * (dprob - delta)).astype(jnp.bfloat16)
    both_grad = dot(dscore, query_wide, NT) + dot(prob_low, grad_wide, NT)
    both_low = both_grad.astype(jnp.bfloat16)
    low = low_ref[...]
    rows, both_rank = low.shape
    spread = [low[at:at + CUT] for at in range(0, rows, CUT)]
    spread.append(jnp.zeros((CUT, LANES - rows // CUT * both_rank), jnp.bfloat16))
    spread = jnp.concatenate(spread, axis=1)
    for block in range(sent_ref.shape[0]):
        sent_ref[block, :rows, :] = both_low[block * rows:(block + 1) * rows]
        sent_ref[block, rows:, :] = spread
    query_grad = dot(both, dscore, TN)
    query_grad_ref[...] = query_grad[:HS].astype(jnp.bfloat16)


def share_kernel(rows, both_rank, sent_ref, got_ref, *out_refs):
    mine = lax.axis_index("dp")
    dp = len(out_refs)
    blocks = sent_ref.shape[0]
    tokens = jnp.concatenate([sent_ref[block, :rows, :] for block in range(blocks)], axis=0)
    lows = []
    for block in range(blocks):
        spread = got_ref[block, rows:, :]
        for at in range(rows // CUT):
            lows.append(spread[:, at * both_rank:(at + 1) * both_rank])
    share = dot(tokens, jnp.concatenate(lows, axis=0), TN)
    column = lax.broadcasted_iota(jnp.int32, (HS, both_rank), 1)
    share = adapter_factor * jnp.where(column < both_rank // 2, share[:HS], share[HS:])
    step = HS // dp
    for s, out_ref in enumerate(out_refs):
        turn = lax.rem(mine + s, dp)
        piece = share[:step]
        for j in range(1, dp):
            piece = jnp.where(turn == j, share[j * step:(j + 1) * step], piece)
        out_ref[...] = piece


def owner_kernel(up_ref, got_ref, key_ref, value_ref, low_grad_ref):
    rows = key_ref.shape[0]
    rank = up_ref.shape[0] // 2
    for pair in range(got_ref.shape[0] // 2):
        first = got_ref[2 * pair, :rows, :]
        second = got_ref[2 * pair + 1, :rows, :]
        columns = slice(2 * pair * HS, (2 * pair + 2) * HS)
        key_ref[:, columns] = jnp.concatenate([first[:, :HS], second[:, :HS]], axis=1)
        value_ref[:, columns] = jnp.concatenate([first[:, HS:], second[:, HS:]], axis=1)
    up = up_ref[...]
    from_key = dot(key_ref[...], up, NT)
    from_value = dot(value_ref[...], up, NT)
    column = lax.broadcasted_iota(jnp.int32, from_key.shape, 1)
    low_grad_ref[...] = adapter_factor * jnp.where(column < rank, from_key, from_value)


def local(dp, mp, query, kv_cache, out_grad, source_lengths, target_lengths, low_rank, adapter_up_matrix):
    tgt_count = query.shape[0]
    rows, both_rank = low_rank.shape
    width = adapter_up_matrix.shape[1]
    step = HS // dp
    vmem = pl.BlockSpec(memory_space=pltpu.VMEM)
    hbm = pl.BlockSpec(memory_space=pl.ANY)
    params = pltpu.CompilerParams(vmem_limit_bytes=48 * 1024 * 1024)
    whole_vmem = pltpu.CompilerParams(vmem_limit_bytes=60 * 1024 * 1024)

    query_t = query.T
    grad_t = out_grad.T
    query_grad_t, sent = pl.pallas_call(
        attention_kernel,
        out_shape=[
            jax.ShapeDtypeStruct((HS, tgt_count), jnp.bfloat16),
            jax.ShapeDtypeStruct((mp, rows + CUT, LANES), jnp.bfloat16),
        ],
        in_specs=[hbm] * 6,
        out_specs=[vmem] * 2,
        scratch_shapes=[
            pltpu.SMEM(source_lengths.shape, jnp.int32),
            pltpu.SMEM(target_lengths.shape, jnp.int32),
            pltpu.VMEM(query_t.shape, jnp.bfloat16),
            pltpu.VMEM(grad_t.shape, jnp.bfloat16),
            pltpu.VMEM(kv_cache.shape, jnp.bfloat16),
            pltpu.VMEM(low_rank.shape, jnp.bfloat16),
            pltpu.SemaphoreType.DMA((6,)),
        ],
        compiler_params=whole_vmem,
        name="attention_backward",
    )(source_lengths, target_lengths, query_t, grad_t, kv_cache, low_rank)

    got = lax.all_to_all(sent, "mp", 0, 0, tiled=True)

    shares = pl.pallas_call(
        functools.partial(share_kernel, rows, both_rank),
        out_shape=[jax.ShapeDtypeStruct((step, both_rank), jnp.float32)] * dp,
        in_specs=[vmem] * 2,
        out_specs=[vmem] * dp,
        compiler_params=params,
        name="adapter_shares",
    )(sent, got)

    up_grad = None
    for s in range(dp):
        route = [(d * mp + h, h * dp + (d + s) % dp) for d in range(dp) for h in range(mp)]
        term = lax.ppermute(shares[s], ("dp", "mp"), route)
        up_grad = term if up_grad is None else up_grad + term

    key_gradient, value_grad, low_grad = pl.pallas_call(
        owner_kernel,
        out_shape=[
            jax.ShapeDtypeStruct((rows, width), jnp.bfloat16),
            jax.ShapeDtypeStruct((rows, width), jnp.bfloat16),
            jax.ShapeDtypeStruct((rows, both_rank), jnp.float32),
        ],
        in_specs=[vmem] * 2,
        out_specs=[vmem] * 3,
        compiler_params=params,
        name="owner_outputs",
    )(adapter_up_matrix, got)
    return query_grad_t.T, key_gradient, value_grad, low_grad, up_grad


def solution(mesh):
    in_specs = (
        P("dp", "mp"),
        P("dp", "mp"),
        P("dp", "mp"),
        P("dp", None),
        P("dp", None),
        P(("dp", "mp"), None),
        P(),
    )
    out_specs = (
        P("dp", "mp"),
        P(("dp", "mp"), None),
        P(("dp", "mp"), None),
        P(("dp", "mp"), None),
        P(("dp", "mp"), None),
    )
    body = functools.partial(local, mesh.shape["dp"], mesh.shape["mp"])
    return jax.shard_map(body, mesh=mesh, in_specs=in_specs, out_specs=out_specs, check_vma=False)
```

profile of v0, /device:TPU:24, one launch (start us, length us, event | category | flops | bytes accessed | tf_op | source)
XLA Modules:
  0.0 26.9 jit_solution(3859385987456698848)
XLA Ops:
  0.6 2.4 %attention_backward.1 = (bf16[64,256]{1,0:T(8,128)(2,1)}, bf16[16,48,128]{2,1,0:T(8,128)(2,1)}) custom-call(s32[1,8]{1,0:T(1,128)} %source_any.1, s32[1,8]{1,0:T(1,128)} %target_any.1, bf16[64,256]{1,0:T(8,128)(2,1)} %bitcast.3, bf16[64,256]{1,0:T(8,128)(2,1)} %bitcast.4, bf16[512,128]{1,0:T(8,128)(2,1)} %kv_any.1, bf16[32,32]{1,0:T(8,128)(2,1)} %low_any.1), custom_call_target="tpu_custom_call" | custom-call | tf_op jit(solution)/shard_map/attention_backward/pallas_call | solution.py:138
  3.1 0.0 copy-start
  3.1 12.3 %all_to_all.5.got_ref = bf16[16,48,128]{2,1,0:T(8,128)(2,1)S(1)} all-to-all(bf16[16,48,128]{2,1,0:T(8,128)(2,1)} %get-tuple-element.13.sent_ref), channel_id=1, replica_groups=mesh['dp'=2,'mp'=16] {'mp'}, dimensions={0} | all-to-all | bytes 393216 | tf_op jit(solution)/shard_map/all_to_all | solution.py:159
  15.4 0.0 copy-done
  15.4 0.0 copy-start.1
  15.4 0.3 adapter_shares.1
  15.6 4.2 %collective-permute-start = (f32[32,32]{1,0:T(8,128)S(1)}, f32[32,32]{1,0:T(8,128)S(1)}, u32[]{:S(2)}, u32[]{:S(2)}) collective-permute-start(f32[32,32]{1,0:T(8,128)S(1)} %get-tuple-element.17), channel_id=1, source_target_pairs={{0,0},{1,2},{2,4},{3,6},{4,8},{5,10},{6,12},{7,14},{8,16},{9,18},{... | collective-permute-start | bytes 12296 | tf_op jit(solution)/shard_map/ppermute | solution.py:173
  19.8 1.3 %collective-permute-start.1 = (f32[32,32]{1,0:T(8,128)S(1)}, f32[32,32]{1,0:T(8,128)S(1)}, u32[]{:S(2)}, u32[]{:S(2)}) collective-permute-start(f32[32,32]{1,0:T(8,128)S(1)} %get-tuple-element.18), channel_id=1, source_target_pairs={{0,1},{1,3},{2,5},{3,7},{4,9},{5,11},{6,13},{7,15},{8,17},{9,19},{... | collective-permute-start | bytes 12296 | tf_op jit(solution)/shard_map/ppermute | solution.py:173
  21.1 0.0 copy-done.1
  21.1 0.9 %owner_outputs.1 = (bf16[32,1024]{1,0:T(8,128)(2,1)}, bf16[32,1024]{1,0:T(8,128)(2,1)}, f32[32,32]{1,0:T(8,128)}) custom-call(bf16[32,1024]{1,0:T(8,128)(2,1)S(1)} %copy-done.1, bf16[16,48,128]{2,1,0:T(8,128)(2,1)S(1)} %all_to_all.5.got_ref), custom_call_target="tpu_custom_call" | custom-call | tf_op jit(solution)/shard_map/owner_outputs/pallas_call | solution.py:176
  22.0 1.1 %collective-permute-done = f32[32,32]{1,0:T(8,128)S(1)} collective-permute-done((f32[32,32]{1,0:T(8,128)S(1)}, f32[32,32]{1,0:T(8,128)S(1)}, u32[]{:S(2)}, u32[]{:S(2)}) %collective-permute-start) | collective-permute-done | bytes 4128 | tf_op jit(solution)/shard_map/ppermute | solution.py:173
  23.1 3.3 %collective-permute-done.1 = f32[32,32]{1,0:T(8,128)S(1)} collective-permute-done((f32[32,32]{1,0:T(8,128)S(1)}, f32[32,32]{1,0:T(8,128)S(1)}, u32[]{:S(2)}, u32[]{:S(2)}) %collective-permute-start.1) | collective-permute-done | bytes 4128 | tf_op jit(solution)/shard_map/ppermute | solution.py:173
  26.3 0.6 %add.3 = f32[32,32]{1,0:T(8,128)} add(f32[32,32]{1,0:T(8,128)S(1)} %collective-permute-done, f32[32,32]{1,0:T(8,128)S(1)} %collective-permute-done.1) | non-fusion elementwise | flops 1024 | bytes 12288 | tf_op jit(solution)/shard_map/add | solution.py:174
Async XLA Ops:
  3.1 12.3 %copy-start = (bf16[16,48,128]{2,1,0:T(8,128)(2,1)S(1)}, bf16[16,48,128]{2,1,0:T(8,128)(2,1)}, u32[]{:S(2)}) copy-start(bf16[16,48,128]{2,1,0:T(8,128)(2,1)} %get-tuple-element.13.sent_ref) | copy-start | bytes 589828
  15.4 5.8 %copy-start.1 = (bf16[32,1024]{1,0:T(8,128)(2,1)S(1)}, bf16[32,1024]{1,0:T(8,128)(2,1)}, u32[]{:S(2)}) copy-start(bf16[32,1024]{1,0:T(8,128)(2,1)} %up_ref.1) | copy-start | bytes 196612
  15.6 7.4 %collective-permute-start = (f32[32,32]{1,0:T(8,128)S(1)}, f32[32,32]{1,0:T(8,128)S(1)}, u32[]{:S(2)}, u32[]{:S(2)}) collective-permute-start(f32[32,32]{1,0:T(8,128)S(1)} %get-tuple-element.17), channel_id=1, source_target_pairs={{0,0},{1,2},{2,4},{3,6},{4,8},{5,10},{6,12},{7,14},{8,16},{9,18},{... | collective-permute-start | bytes 12296 | tf_op jit(solution)/shard_map/ppermute | solution.py:173
  19.8 6.5 %collective-permute-start.1 = (f32[32,32]{1,0:T(8,128)S(1)}, f32[32,32]{1,0:T(8,128)S(1)}, u32[]{:S(2)}, u32[]{:S(2)}) collective-permute-start(f32[32,32]{1,0:T(8,128)S(1)} %get-tuple-element.18), channel_id=1, source_target_pairs={{0,1},{1,3},{2,5},{3,7},{4,9},{5,11},{6,13},{7,15},{8,17},{9,19},{... | collective-permute-start | bytes 12296 | tf_op jit(solution)/shard_map/ppermute | solution.py:173
where the time goes:
time: 27.2 us; the launch traced here: 26.9 us
  blocking collectives  12.3 us (45%)
  starting transfers between devices  5.49 us (20%)
  waiting for transfers between devices  4.33 us (16%)
  Pallas kernels  3.54 us (13%)
  between operations  0.67 us (2%)
  other arithmetic  0.61 us (2%)
    all_to_all x1, blocking collectives, local(): got = lax.all_to_all(sent, 'mp', 0, 0, tiled=True)  12.3 us
    ppermute x2, starting transfers between devices, local(): term = lax.ppermute(shares[s], ('dp', 'mp'), route)  5.49 us
    ppermute x2, waiting for transfers between devices, local(): term = lax.ppermute(shares[s], ('dp', 'mp'), route)  4.33 us
    pallas_call x1, Pallas kernels, local(): pl.pallas_call(attention_kernel, out_shape=[jax.ShapeDtypeStruct((HS, tgt...  2.42 us
    pallas_call x1, Pallas kernels, local(): pl.pallas_call(owner_kernel, out_shape=[jax.ShapeDtypeStruct((rows, width...  0.86 us
    add x1, other arithmetic, local(): up_grad = term if up_grad is None else up_grad + term  0.61 us
  transfers between devices with their start and end apart: 2, of which 2 were waited for; matrix products, arithmetic and copies ran while one was open for 0% of the time, Pallas kernels for 3%

commit v1 on v0

--- a/solution.py
+++ b/solution.py
@@ -19,6 +19,20 @@
 
 def dot(left, right, dims):
     return lax.dot_general(left, right, dims, preferred_element_type=jnp.float32)
+
+
+def group_order(count):
+    quarter = count // 4
+    bits = quarter.bit_length() - 1
+    assert count == 4 << bits
+    turned = [sum(((i >> b) & 1) << (bits - 1 - b) for b in range(bits)) for i in range(quarter)]
+    order = []
+    for low, high in ((1, 2), (0, 3)):
+        for i in range(0, quarter, 2):
+            first, second = turned[i], turned[i + 1]
+            order += [low * quarter + first, high * quarter + second]
+            order += [low * quarter + second, high * quarter + first]
+    return order
 
 
 def source_range(source_ref, target_ref, count):
@@ -78,9 +92,9 @@
     spread = [low[at:at + CUT] for at in range(0, rows, CUT)]
     spread.append(jnp.zeros((CUT, LANES - rows // CUT * both_rank), jnp.bfloat16))
     spread = jnp.concatenate(spread, axis=1)
-    for block in range(sent_ref.shape[0]):
-        sent_ref[block, :rows, :] = both_low[block * rows:(block + 1) * rows]
-        sent_ref[block, rows:, :] = spread
+    for at, block in enumerate(group_order(sent_ref.shape[0])):
+        sent_ref[at, :rows, :] = both_low[block * rows:(block + 1) * rows]
+        sent_ref[at, rows:, :] = spread
     query_grad = dot(both, dscore, TN)
     query_grad_ref[...] = query_grad[:HS].astype(jnp.bfloat16)
 
@@ -110,9 +124,10 @@
 def owner_kernel(up_ref, got_ref, key_ref, value_ref, low_grad_ref):
     rows = key_ref.shape[0]
     rank = up_ref.shape[0] // 2
-    for pair in range(got_ref.shape[0] // 2):
-        first = got_ref[2 * pair, :rows, :]
-        second = got_ref[2 * pair + 1, :rows, :]
+    order = group_order(got_ref.shape[0])
+    for pair in range(len(order) // 2):
+        first = got_ref[order.index(2 * pair), :rows, :]
+        second = got_ref[order.index(2 * pair + 1), :rows, :]
         columns = slice(2 * pair * HS, (2 * pair + 2) * HS)
         key_ref[:, columns] = jnp.concatenate([first[:, :HS], second[:, :HS]], axis=1)
         value_ref[:, columns] = jnp.concatenate([first[:, HS:], second[:, HS:]], axis=1)
@@ -156,7 +171,7 @@
         name="attention_backward",
     )(source_lengths, target_lengths, query_t, grad_t, kv_cache, low_rank)
 
-    got = lax.all_to_all(sent, "mp", 0, 0, tiled=True)
+    got = lax.all_to_all(sent, "mp", 0, 0, axis_index_groups=[group_order(mp)], tiled=True)
 
     shares = pl.pallas_call(
         functools.partial(share_kernel, rows, both_rank),

time: 27.2 us -> 26.3 us (0.967)
  the two profiles are of different devices: /device:TPU:24 before, /device:TPU:16 now
where the time goes in v1:
time: 26.3 us; the launch traced here: 26 us
  blocking collectives  11.7 us (44%)
  starting transfers between devices  5.68 us (22%)
  waiting for transfers between devices  3.76 us (14%)
  Pallas kernels  3.54 us (13%)
  between operations  0.68 us (3%)
  other arithmetic  0.61 us (2%)
    all_to_all x1, blocking collectives, local(): lax.all_to_all(sent, 'mp', 0, 0, axis_index_groups=[group_order(mp)], til...  11.7 us
    ppermute x2, starting transfers between devices, local(): term = lax.ppermute(shares[s], ('dp', 'mp'), route)  5.68 us
    ppermute x2, waiting for transfers between devices, local(): term = lax.ppermute(shares[s], ('dp', 'mp'), route)  3.76 us
    pallas_call x1, Pallas kernels, local(): pl.pallas_call(attention_kernel, out_shape=[jax.ShapeDtypeStruct((HS, tgt...  2.42 us
    pallas_call x1, Pallas kernels, local(): pl.pallas_call(owner_kernel, out_shape=[jax.ShapeDtypeStruct((rows, width...  0.85 us
    add x1, other arithmetic, local(): up_grad = term if up_grad is None else up_grad + term  0.61 us
  transfers between devices with their start and end apart: 2, of which 2 were waited for; matrix products, arithmetic and copies ran while one was open for 0% of the time, Pallas kernels for 3%

profile of v1, /device:TPU:16, one launch (start us, length us, event | category | flops | bytes accessed | tf_op | source)
XLA Modules:
  0.0 26.0 jit_solution(18397768949576724144)
XLA Ops:
  0.6 2.4 %attention_backward.1 = (bf16[64,256]{1,0:T(8,128)(2,1)}, bf16[16,48,128]{2,1,0:T(8,128)(2,1)}) custom-call(s32[1,8]{1,0:T(1,128)} %source_any.1, s32[1,8]{1,0:T(1,128)} %target_any.1, bf16[64,256]{1,0:T(8,128)(2,1)} %bitcast.3, bf16[64,256]{1,0:T(8,128)(2,1)} %bitcast.4, bf16[512,128]{1,0:T(8,128)(2,1)} %kv_any.1, bf16[32,32]{1,0:T(8,128)(2,1)} %low_any.1), custom_call_target="tpu_custom_call" | custom-call | tf_op jit(solution)/shard_map/attention_backward/pallas_call | solution.py:153
  3.1 0.0 copy-start
  3.1 11.7 %all_to_all.5.got_ref = bf16[16,48,128]{2,1,0:T(8,128)(2,1)S(1)} all-to-all(bf16[16,48,128]{2,1,0:T(8,128)(2,1)} %get-tuple-element.13.sent_ref), channel_id=1, replica_groups={{4,10,6,8,5,11,7,9,0,14,2,12,1,15,3,13},{20,26,22,24,21,27,23,25,16,30,..., dimensions={0} | all-to-all | bytes 393216 | tf_op jit(solution)/shard_map/all_to_all | solution.py:174
  14.8 0.0 copy-done
  14.8 0.0 copy-start.1
  14.8 0.3 %adapter_shares.1 = (f32[32,32]{1,0:T(8,128)S(1)}, f32[32,32]{1,0:T(8,128)S(1)}) custom-call(bf16[16,48,128]{2,1,0:T(8,128)(2,1)S(1)} %copy-done, bf16[16,48,128]{2,1,0:T(8,128)(2,1)S(1)} %all_to_all.5.got_ref), custom_call_target="tpu_custom_call" | custom-call | tf_op jit(solution)/shard_map/adapter_shares/pallas_call | solution.py:176
  15.1 5.6 %collective-permute-start = (f32[32,32]{1,0:T(8,128)S(1)}, f32[32,32]{1,0:T(8,128)S(1)}, u32[]{:S(2)}, u32[]{:S(2)}) collective-permute-start(f32[32,32]{1,0:T(8,128)S(1)} %get-tuple-element.17), channel_id=1, source_target_pairs={{0,0},{1,2},{2,4},{3,6},{4,8},{5,10},{6,12},{7,14},{8,16},{9,18},{... | collective-permute-start | bytes 12296 | tf_op jit(solution)/shard_map/ppermute | solution.py:188
  20.7 0.1 collective-permute-start.1
  20.8 0.0 copy-done.1
  20.8 0.9 %owner_outputs.1 = (bf16[32,1024]{1,0:T(8,128)(2,1)}, bf16[32,1024]{1,0:T(8,128)(2,1)}, f32[32,32]{1,0:T(8,128)}) custom-call(bf16[32,1024]{1,0:T(8,128)(2,1)S(1)} %copy-done.1, bf16[16,48,128]{2,1,0:T(8,128)(2,1)S(1)} %all_to_all.5.got_ref), custom_call_target="tpu_custom_call" | custom-call | tf_op jit(solution)/shard_map/owner_outputs/pallas_call | solution.py:191
  21.6 0.5 %collective-permute-done = f32[32,32]{1,0:T(8,128)S(1)} collective-permute-done((f32[32,32]{1,0:T(8,128)S(1)}, f32[32,32]{1,0:T(8,128)S(1)}, u32[]{:S(2)}, u32[]{:S(2)}) %collective-permute-start) | collective-permute-done | bytes 4128 | tf_op jit(solution)/shard_map/ppermute | solution.py:188
  22.1 3.3 %collective-permute-done.1 = f32[32,32]{1,0:T(8,128)S(1)} collective-permute-done((f32[32,32]{1,0:T(8,128)S(1)}, f32[32,32]{1,0:T(8,128)S(1)}, u32[]{:S(2)}, u32[]{:S(2)}) %collective-permute-start.1) | collective-permute-done | bytes 4128 | tf_op jit(solution)/shard_map/ppermute | solution.py:188
  25.4 0.6 %add.3 = f32[32,32]{1,0:T(8,128)} add(f32[32,32]{1,0:T(8,128)S(1)} %collective-permute-done, f32[32,32]{1,0:T(8,128)S(1)} %collective-permute-done.1) | non-fusion elementwise | flops 1024 | bytes 12288 | tf_op jit(solution)/shard_map/add | solution.py:189
Async XLA Ops:
  3.1 11.7 %copy-start = (bf16[16,48,128]{2,1,0:T(8,128)(2,1)S(1)}, bf16[16,48,128]{2,1,0:T(8,128)(2,1)}, u32[]{:S(2)}) copy-start(bf16[16,48,128]{2,1,0:T(8,128)(2,1)} %get-tuple-element.13.sent_ref) | copy-start | bytes 589828
  14.8 6.0 %copy-start.1 = (bf16[32,1024]{1,0:T(8,128)(2,1)S(1)}, bf16[32,1024]{1,0:T(8,128)(2,1)}, u32[]{:S(2)}) copy-start(bf16[32,1024]{1,0:T(8,128)(2,1)} %up_ref.1) | copy-start | bytes 196612
  15.1 7.0 %collective-permute-start = (f32[32,32]{1,0:T(8,128)S(1)}, f32[32,32]{1,0:T(8,128)S(1)}, u32[]{:S(2)}, u32[]{:S(2)}) collective-permute-start(f32[32,32]{1,0:T(8,128)S(1)} %get-tuple-element.17), channel_id=1, source_target_pairs={{0,0},{1,2},{2,4},{3,6},{4,8},{5,10},{6,12},{7,14},{8,16},{9,18},{... | collective-permute-start | bytes 12296 | tf_op jit(solution)/shard_map/ppermute | solution.py:188
  20.7 4.7 %collective-permute-start.1 = (f32[32,32]{1,0:T(8,128)S(1)}, f32[32,32]{1,0:T(8,128)S(1)}, u32[]{:S(2)}, u32[]{:S(2)}) collective-permute-start(f32[32,32]{1,0:T(8,128)S(1)} %get-tuple-element.18), channel_id=1, source_target_pairs={{0,1},{1,3},{2,5},{3,7},{4,9},{5,11},{6,13},{7,15},{8,17},{9,19},{... | collective-permute-start | bytes 12296 | tf_op jit(solution)/shard_map/ppermute | solution.py:188
